TPU v7x, 512 devices: a whole 4x4x16 slice. The times are simulated.
512 devices in a mesh: head: 16 (over z_hi, x, core), ctx: 32 (over z_lo, y).
Axes of the slice: x: 4, y: 4, z: 16 (z_hi: 2, z_lo: 8; z = z_hi * 8 + z_lo), core: 2. Of those that a mesh axis runs over, the one named last changes fastest.
Arguments:
- queries: bfloat16 [4096, 128, 128], P('ctx', 'head'), may hold values from -8 to 8
- keys: bfloat16 [4096, 1024], P('ctx', 'head'), may hold values from -8 to 8
- values: bfloat16 [4096, 1024], P('ctx', 'head'), may hold values from -6 to 6
- stretch_order: int32 [32, 2], replicated, may hold values from 0 to 63, as said below
Outputs:
- attended: bfloat16 [4096, 128, 128], P('ctx', 'head')
Inputs may be any that keep to these rules, and one draw needn't show every extreme that they name: `stretch_order`: every stretch 0 to 63 stands exactly once in the table, and the two stretches of a row add up to 63.
All inputs are finite; a program needn't handle non-finite values.
Results may differ from a plain program's by a relative error of at most 0.035.
Values may be sent and summed in bfloat16 or wider, within the bound.
A program may use at most 64 MiB of HBM per device.

v0:
```python
import jax
import jax.numpy as jnp
from jax import lax
from jax.sharding import PartitionSpec as P


def from_partner(value, axis, bit):
    return lax.ppermute(value, axis, [(i, i ^ 1 << bit) for i in range(lax.axis_size(axis))])


def row_positions(rows, table, stretch):
    blocks = rows // stretch
    onehot = blocks[:, None] == jnp.arange(table.shape[0], dtype=jnp.int32)[None, :]
    starts = jnp.sum(jnp.where(onehot, table[None, :], 0), axis=1)
    return starts * stretch + rows % stretch


def partials(query_rows, query_pos, key_rows, value_rows, key_pos):
    scale = query_rows.shape[-1] ** (-0.5)
    scores = (
        jnp.einsum("rhd,ntd->nrht", query_rows, key_rows, preferred_element_type=jnp.float32)
        * scale
    )
    visible = key_pos[:, None, None, :] <= query_pos[None, :, None, None]
    scores = jnp.where(visible, scores, jnp.float32(-1e30))
    top = jnp.max(scores, axis=-1)
    weights = jnp.exp(scores - top[..., None])
    total = jnp.sum(weights, axis=-1)
    rounded = weights.astype(jnp.bfloat16)
    mixed = jnp.einsum("nrht,ntd->nrhd", rounded, value_rows, preferred_element_type=jnp.float32)
    mixed = (mixed / total[..., None]).astype(jnp.bfloat16)
    return (mixed, top + jnp.log(total))


def shards(queries, keys, values, stretch_order):
    table = stretch_order.reshape(-1)
    tokens = queries.shape[0]
    heads = queries.shape[1]
    width = queries.shape[2]
    stretch = tokens // 2
    local_rows = lax.axis_index("ctx") * tokens + jnp.arange(tokens, dtype=jnp.int32)
    local_pos = row_positions(local_rows, table, stretch)
    other_keys, other_values = from_partner((keys, values), "head", 0)
    upper = lax.axis_index("head") % 2 == 1
    head_keys = jnp.where(
        upper,
        jnp.concatenate([other_keys, keys], axis=1),
        jnp.concatenate([keys, other_keys], axis=1),
    )
    head_values = jnp.where(
        upper,
        jnp.concatenate([other_values, values], axis=1),
        jnp.concatenate([values, other_values], axis=1),
    )
    run_top = jnp.full((tokens, heads), -1e30, jnp.float32)
    key_piece = lax.all_gather(head_keys, "ctx", axis=0, tiled=True)
    value_piece = lax.all_gather(head_values, "ctx", axis=0, tiled=True)
    count = key_piece.shape[0] // tokens
    rows = jnp.arange(key_piece.shape[0], dtype=jnp.int32)
    key_pos = row_positions(rows, table, stretch).reshape(count, tokens)
    mixed, lse = partials(
        queries,
        local_pos,
        key_piece.reshape(count, tokens, width),
        value_piece.reshape(count, tokens, width),
        key_pos,
    )
    new_top = jnp.maximum(run_top, jnp.max(lse, axis=0))
    share = jnp.exp(lse - new_top[None])
    new_total = jnp.sum(share, axis=0)
    new_acc = jnp.sum(share[..., None] * mixed.astype(jnp.float32), axis=0)
    return (new_acc / new_total[..., None]).astype(jnp.bfloat16)


def solution(mesh):
    in_specs = (P("ctx", "head", None), P("ctx", "head"), P("ctx", "head"), P())
    out_specs = P("ctx", "head", None)
    return jax.shard_map(shards, mesh=mesh, in_specs=in_specs, out_specs=out_specs, check_vma=False)
```

profile of v0, /device:TPU:4, one launch (start us, length us, event | category | flops | bytes accessed | tf_op | source)
XLA Modules:
  0.0 390.1 jit_solution(16360264001809663246)
XLA Ops:
  6.5 0.0 all-gather.3.cloned.1.call-start
  6.5 1.9 collective-permute-start
  8.5 1.3 collective-permute-done
  9.8 1.4 maximum_select_fusion
  11.2 0.0 all-gather.3.cloned.1.call-update
  11.3 0.0 all-gather.5.cloned.1.call-start
  11.3 2.1 collective-permute-start.1
  13.4 0.8 copy.21
  14.2 0.1 broadcast_in_dim.51
  14.3 0.1 select_reduce_fusion.1
  14.4 0.2 select_reduce_fusion
  14.7 0.7 broadcast_compare_fusion
  15.4 0.0 collective-permute-done.1
  15.4 1.4 maximum_select_fusion.1
  16.8 0.0 all-gather.5.cloned.1.call-update
  16.8 176.8 %all-gather.3.cloned.1.call-done = bf16[4096,128]{0,1:T(8,128)(2,1)} async-done(((bf16[128,128]{0,1:T(8,128)(2,1)}), bf16[4096,128]{0,1:T(8,128)(2,1)}) %all-gather.3.cloned.1.call-update) | async-done | bytes 1048592 | tf_op jit(solution)/shard_map/all_gather | solution.py:56
  193.6 1.6 copy.22
  195.2 8.1 %fusion.2 = (f32[32,128,8]{1,2,0:T(8,128)S(1)}, f32[32,128,128,8]{2,1,3,0:T(8,128)}) fusion(pred[32,128,128]{1,2,0:T(8,128)(4,1)S(1)} %broadcast_compare_fusion, bf16[32,128,128,1]{2,1,3,0:T(8,128)(2,1)S(1)} %bitcast.30, bf16[128,8,128]{2,1,0:T(8,128)(2,1)} %param.4), kind=kOutput, calls=%fused_computation.6 | convolution fusion | flops 1086291968 | bytes 18743296 | tf_op jit(solution)/shard_map/rhd,ntd->nrht/dot_general | solution.py:21
  203.3 10.5 %fusion.1 = f32[32,128,8]{1,2,0:T(8,128)S(1)} fusion(f32[32,128,128,8]{2,1,3,0:T(8,128)} %get-tuple-element.8, f32[32,128,8]{1,2,0:T(8,128)S(1)} %get-tuple-element.7, pred[32,128,128]{1,2,0:T(8,128)(4,1)S(1)} %broadcast_compare_fusion), kind=kLoop, calls=%fused_computation.5 | loop fusion | flops 16744448 | bytes 17563648 | tf_op jit(solution)/shard_map/reduce_sum | solution.py:28
  213.9 0.1 fusion.14
  213.9 151.6 %all-gather.5.cloned.1.call-done = bf16[4096,128]{0,1:T(8,128)(2,1)} async-done(((bf16[128,128]{0,1:T(8,128)(2,1)}), bf16[4096,128]{0,1:T(8,128)(2,1)}) %all-gather.5.cloned.1.call-update) | async-done | bytes 1048592 | tf_op jit(solution)/shard_map/all_gather | solution.py:57
  365.6 1.6 copy.24
  367.2 14.9 %multiply_reduce_fusion = f32[128,8,128]{2,0,1:T(8,128)S(1)} fusion(f32[32,128,8]{1,2,0:T(8,128)S(1)} %get-tuple-element.6, f32[32,128,8]{1,2,0:T(8,128)S(1)} %fusion.1, bf16[32,128,128,1]{2,1,3,0:T(8,128)(2,1)S(1)} %bitcast.31, f32[32,128,128,8]{2,1,3,0:T(8,128)} %get-tuple-element.8, f32[32,128,8]{1,2,0:T(8,128)S(1)} %get-tuple-element.7, ...), kind=kOutput, calls=%fused_computation.1 | convolution fusion | flops 1111359488 | bytes 19267584 | tf_op jit(solution)/shard_map/nrht,ntd->nrhd/dot_general | solution.py:30
  382.2 0.2 divide_convert_fusion.1
  382.4 0.9 copy.26
  (6 shorter events, 0.1 us)
Async XLA Ops:
  6.5 187.1 %all-gather.3.cloned.1.call-start = ((), (), s32[]{:S(2)}) async-start(), calls=%async_computation | async-start | bytes 1081344 | tf_op jit(solution)/shard_map/all_gather | solution.py:56
  6.5 3.3 collective-permute-start
  11.3 354.3 %all-gather.5.cloned.1.call-start = ((), (), s32[]{:S(2)}) async-start(), calls=%async_computation.1 | async-start | bytes 1081344 | tf_op jit(solution)/shard_map/all_gather | solution.py:57
  11.3 4.1 %collective-permute-start.1 = (bf16[128,64]{0,1:T(8,128)(2,1)}, bf16[128,64]{0,1:T(8,128)(2,1)S(1)}, u32[]{:S(2)}, u32[]{:S(2)}) collective-permute-start(bf16[128,64]{0,1:T(8,128)(2,1)} %param.6), channel_id=1, source_target_pairs={{0,32},{32,0},{64,96},{96,64},{128,160},{160,128},{192,224},{224,1... | collective-permute-start | bytes 49160 | tf_op jit(solution)/shard_map/ppermute | solution.py:8
Sparse Core Ops, SparseCore 0:
  11.4 182.2 all-gather.2
  195.6 169.9 all-gather.4
where the time goes:
time: 391 us; the launch traced here: 390 us
  waiting for transfers between devices  330 us (84%)
  matrix products  23 us (6%)
  other arithmetic  14.7 us (4%)
  between operations  13.5 us (3%)
  local copies, waits for them, and re-layouts  4.96 us (1%)
  starting transfers between devices  4.03 us (1%)
    all_gather x1, waiting for transfers between devices, shards(): key_piece = lax.all_gather(head_keys, 'ctx', axis=0, tiled=True)  177 us
    all_gather x1, waiting for transfers between devices, shards(): value_piece = lax.all_gather(head_values, 'ctx', axis=0, tiled=True)  152 us
    dot_general x1, matrix products, partials(): jnp.einsum('nrht,ntd->nrhd', rounded, value_rows, preferred_element_type=...  14.9 us
    reduce_sum x1, other arithmetic, partials(): total = jnp.sum(weights, axis=-1)  10.5 us
    dot_general x1, matrix products, partials(): jnp.einsum('rhd,ntd->nrht', query_rows, key_rows, preferred_element_type=...  8.09 us
  transfers between devices with their start and end apart: 4, of which 3 were waited for; matrix products, arithmetic and copies ran while one was open for 6% of the time, Pallas kernels for 0%

commit v1 on v0

v1 whole, which is shorter than its diff:
```python
import functools
import math

import jax
import jax.numpy as jnp
from jax import lax
from jax.experimental import pallas as pl
from jax.experimental.pallas import tpu as pltpu
from jax.sharding import PartitionSpec as P

MESH = pl.DeviceIdType.MESH
NEG = -1e30


def along_y(s):
    return [("send", s, 1), ("send", s, 3), ("send", s, 2)]


def along_z(s):
    return [("send", s, 12), ("send", s, 8), ("send", s, 4)]


def swap(g):
    return [("swap", 4 * g, 4)]


def attend(g):
    return [("attend", g)]


PROGRAM = (
    [("send", 0, 16)] + along_z(0) + along_y(0)
    + along_y(4) + along_y(8) + along_y(12) + swap(0)
    + along_z(16) + along_y(16) + attend(0)
    + swap(1) + swap(2) + swap(3)
    + attend(1)
    + along_y(20) + along_y(24) + along_y(28)
    + attend(2) + attend(3)
    + swap(4) + attend(4) + swap(5) + swap(6) + attend(5) + swap(7) + attend(6) + attend(7)
)
SENDS = sum(op[0] == "send" for op in PROGRAM)
SWAPS = sum(op[0] == "swap" for op in PROGRAM)


def kernel(
    q_hbm, k_ref, v_ref, table, out_ref,
    q_raw, q_wide, mine, theirs, bias, top, total, acc,
    q_sem, send_sem, recv_sem, swap_send, swap_recv,
):
    h = lax.axis_index("head")
    c = lax.axis_index("ctx")
    tokens = k_ref.shape[0]
    half = k_ref.shape[1]
    width = 2 * half
    rows = q_raw.shape[0]
    heads = rows // tokens
    stretch = tokens // 2
    upper = h % 2 == 1
    keys = 4 * tokens
    factor = width ** (-0.5) * math.log2(math.e)

    q_copy = pltpu.make_async_copy(q_hbm, q_raw, q_sem)
    q_copy.start()
    jumps = sorted({op[2] for op in PROGRAM if op[0] == "send"}, reverse=True)
    barrier = pltpu.get_barrier_semaphore()
    for k in jumps:
        pl.semaphore_signal(barrier, inc=1, device_id=(h, c ^ k), device_id_type=MESH)
    pl.semaphore_signal(barrier, inc=1, device_id=(h ^ 1, c), device_id_type=MESH)

    kk, vv = k_ref[...], v_ref[...]
    mine[0] = jnp.where(
        upper, jnp.concatenate([kk, vv], axis=1), jnp.concatenate([vv, kk], axis=1)
    )
    pl.semaphore_wait(barrier, len(jumps) + 1)

    def remote(s, k, i):
        return pltpu.make_async_remote_copy(
            src_ref=mine.at[s], dst_ref=mine.at[s ^ k],
            send_sem=send_sem.at[i], recv_sem=recv_sem.at[s ^ k],
            device_id=(h, c ^ k), device_id_type=MESH,
        )

    def across(s, n, i):
        part = pl.ds(s, n)
        return pltpu.make_async_remote_copy(
            src_ref=mine.at[part], dst_ref=theirs.at[part],
            send_sem=swap_send.at[i], recv_sem=swap_recv.at[i],
            device_id=(h ^ 1, c), device_id_type=MESH,
        )

    def prepare():
        q_copy.wait()
        lane = lax.broadcasted_iota(jnp.int32, (1, width), 1)
        low = lane < half
        raw = q_raw[...].astype(jnp.float32)
        rolled = jnp.concatenate([raw[:, half:], raw[:, :half]], axis=1)
        left = jnp.where(low, rolled, 0.0)
        right = jnp.where(low, 0.0, rolled)
        q_wide[:, :width] = jnp.where(upper, left, right).astype(jnp.bfloat16)
        q_wide[:, width:] = jnp.where(upper, right, left).astype(jnp.bfloat16)
        for s in range(mine.shape[0]):
            b = c ^ s
            held = jnp.where(low, table[b, 0], table[b, 1])
            for a in range(2):
                bias[a, s // 4 : s // 4 + 1, (s % 4) * tokens : (s % 4 + 1) * tokens] = jnp.where(
                    held < table[c, a], 0.0, NEG
                )

    def group(g):
        part = pl.ds(4 * g, 4)
        return jnp.concatenate(
            [mine[part].reshape(keys, width), theirs[part].reshape(keys, width)], axis=1
        )

    def step(g, a):
        span = pl.ds(a * (rows // 2), rows // 2)
        kv = group(g)
        scores = lax.dot_general(
            q_wide[span, :], kv, (((1,), (1,)), ((), ())), preferred_element_type=jnp.float32
        )
        shut = bias[pl.ds(a, 1), g : g + 1, :].reshape(1, keys)
        if g == 0:
            lane = lax.broadcasted_iota(jnp.int32, (1, tokens), 1)
            held = jnp.where(
                lane < stretch, table[c, 0] * stretch + lane, table[c, 1] * stretch + lane - stretch
            )
            row = lax.broadcasted_iota(jnp.int32, (rows // 2, 1), 0) // heads
            seen = held <= table[c, a] * stretch + row
            own = jnp.where(seen, scores[:, :tokens], NEG)
            scores = jnp.concatenate([own, scores[:, tokens:] + shut[:, tokens:]], axis=1)
            new_top = jnp.max(scores, axis=1, keepdims=True)
        else:
            scores = scores + shut
            old_top = top[span, :1]
            new_top = jnp.maximum(old_top, jnp.max(scores, axis=1, keepdims=True))
        weights = jnp.exp2((scores - new_top) * factor)
        partial = (
            weights[:, :tokens] + weights[:, tokens : 2 * tokens]
            + weights[:, 2 * tokens : 3 * tokens] + weights[:, 3 * tokens :]
        )
        mixed = jnp.dot(weights.astype(jnp.bfloat16), kv, preferred_element_type=jnp.float32)
        if g == 0:
            total[span, :] = partial
            acc[span, :] = mixed
        else:
            fade = jnp.exp2((old_top - new_top) * factor)
            total[span, :] = total[span, :] * fade + partial
            acc[span, :] = acc[span, :] * fade + mixed
        top[span, :] = jnp.broadcast_to(new_top, (rows // 2, tokens))

    here = {0}

    def arrived(s):
        if s not in here:
            here.add(s)
            remote(s ^ 1, 1, 0).wait_recv()

    sent, swapped, swap_of = [], [], {}
    first = True
    for op in PROGRAM:
        if op[0] == "send":
            arrived(op[1])
            sent.append(remote(op[1], op[2], len(sent)))
            sent[-1].start()
            if first and len(sent) == len(jumps):
                prepare()
                first = False
        elif op[0] == "swap":
            for s in range(op[1], op[1] + op[2]):
                arrived(s)
                swap_of[s] = len(swapped)
            swapped.append(across(op[1], op[2], len(swapped)))
            swapped[-1].start()
        else:
            g = op[1]
            swapped[swap_of[4 * g]].wait_recv()

            def body(a, carry, g=g):
                step(g, a)
                return carry

            lax.fori_loop(0, 2, body, 0)

    whole = jnp.sum(total[...], axis=1, keepdims=True)
    lane = lax.broadcasted_iota(jnp.int32, (1, width), 1)
    pick = (lane < half) != upper
    mix = jnp.where(pick, acc[:, :width], acc[:, width:])
    out_ref[...] = (mix / whole).astype(out_ref.dtype)
    for copy in sent + swapped:
        copy.wait_send()


def shards(queries, keys, values, stretch_order):
    tokens, heads, width = queries.shape
    rows = tokens * heads
    blocks = lax.axis_size("ctx")
    vmem = pl.BlockSpec(memory_space=pltpu.VMEM)
    out = pl.pallas_call(
        kernel,
        out_shape=jax.ShapeDtypeStruct((rows, width), queries.dtype),
        in_specs=[
            pl.BlockSpec(memory_space=pl.ANY), vmem, vmem,
            pl.BlockSpec(memory_space=pltpu.SMEM),
        ],
        out_specs=vmem,
        scratch_shapes=[
            pltpu.VMEM((rows, width), jnp.bfloat16),
            pltpu.VMEM((rows, 2 * width), jnp.bfloat16),
            pltpu.VMEM((blocks, tokens, width), jnp.bfloat16),
            pltpu.VMEM((blocks, tokens, width), jnp.bfloat16),
            pltpu.VMEM((2, blocks // 4, 4 * tokens), jnp.float32),
            pltpu.VMEM((rows, tokens), jnp.float32),
            pltpu.VMEM((rows, tokens), jnp.float32),
            pltpu.VMEM((rows, 2 * width), jnp.float32),
            pltpu.SemaphoreType.DMA,
            pltpu.SemaphoreType.DMA((SENDS,)),
            pltpu.SemaphoreType.DMA((blocks,)),
            pltpu.SemaphoreType.DMA((SWAPS,)),
            pltpu.SemaphoreType.DMA((SWAPS,)),
        ],
        compiler_params=pltpu.CompilerParams(
            collective_id=0, has_side_effects=True, vmem_limit_bytes=48 * 1024 * 1024
        ),
    )(queries.reshape(rows, width), keys, values, stretch_order)
    return out.reshape(tokens, heads, width)


def solution(mesh):
    in_specs = (P("ctx", "head", None), P("ctx", "head"), P("ctx", "head"), P())
    out_specs = P("ctx", "head", None)
    return jax.shard_map(shards, mesh=mesh, in_specs=in_specs, out_specs=out_specs, check_vma=False)
```

time: 391 us -> 48.4 us (0.12)
  the two profiles are of different devices: /device:TPU:4 before, /device:TPU:66 now
where the time goes in v1:
time: 48.4 us; the launch traced here: 48.1 us
  Pallas kernels  44.8 us (93%)
  local copies, waits for them, and re-layouts  3.25 us (7%)
    pallas_call x1, Pallas kernels, shards(): pl.pallas_call(kernel, out_shape=jax.ShapeDtypeStruct((rows, width), quer...  44.8 us
    unnamed x12, local copies, waits for them, and re-layouts  3.25 us

profile of v1, /device:TPU:66, one launch (start us, length us, event | category | flops | bytes accessed | tf_op | source)
XLA Modules:
  0.0 48.1 jit_solution(526853843110861574)
XLA Ops:
  0.0 0.0 copy-start.3
  0.0 0.0 copy-start.1
  0.0 0.7 %copy-done.3 = s32[32,2]{0,1:T(2,128)S(1)} copy-done((s32[32,2]{0,1:T(2,128)S(1)}, s32[32,2]{0,1:T(2,128)}, u32[]{:S(2)}) %copy-start.3) | copy-done | bytes 280
  0.7 0.1 copy.7.table
  0.8 0.0 copy-done.1
  0.8 0.0 copy-start.2
  0.8 0.1 copy.5.k_ref
  0.9 0.6 %copy-done.2 = bf16[128,64]{0,1:T(8,128)(2,1)S(1)} copy-done((bf16[128,64]{0,1:T(8,128)(2,1)S(1)}, bf16[128,64]{0,1:T(8,128)(2,1)}, u32[]{:S(2)}) %copy-start.2) | copy-done | bytes 16408
  1.5 0.1 copy.6.v_ref
  1.6 0.0 copy-start
  1.6 0.9 %copy-done = bf16[128,8,128]{2,1,0:T(8,128)(2,1)S(1)} copy-done((bf16[128,8,128]{2,1,0:T(8,128)(2,1)S(1)}, bf16[128,8,128]{2,1,0:T(8,128)(2,1)}, u32[]{:S(2)}) %copy-start) | copy-done | bytes 262168
  2.6 44.8 %shard_map.46 = bf16[1024,128]{1,0:T(8,128)(2,1)S(1)} custom-call(bf16[1024,128]{1,0:T(8,128)(2,1)S(1)} %bitcast.3, bf16[128,64]{1,0:T(8,128)(2,1)S(1)} %copy.5.k_ref, bf16[128,64]{1,0:T(8,128)(2,1)S(1)} %copy.6.v_ref, s32[32,2]{1,0:T(8,128)S(1)} %copy.7.table), custom_call_target="tpu_custom_call" | custom-call | tf_op jit(solution)/shard_map/pallas_call | solution.py:198
  47.4 0.7 %copy.9 = bf16[128,8,128]{2,1,0:T(8,128)(2,1)} copy(bf16[128,8,128]{2,1,0:T(8,128)(2,1)S(1)} %bitcast.2) | data formatting | bytes 524288
Async XLA Ops:
  0.0 0.7 %copy-start.3 = (s32[32,2]{0,1:T(2,128)S(1)}, s32[32,2]{0,1:T(2,128)}, u32[]{:S(2)}) copy-start(s32[32,2]{0,1:T(2,128)} %param.7) | copy-start | bytes 772
  0.0 0.8 %copy-start.1 = (bf16[128,64]{0,1:T(8,128)(2,1)S(1)}, bf16[128,64]{0,1:T(8,128)(2,1)}, u32[]{:S(2)}) copy-start(bf16[128,64]{0,1:T(8,128)(2,1)} %param.5) | copy-start | bytes 49156
  0.8 0.7 %copy-start.2 = (bf16[128,64]{0,1:T(8,128)(2,1)S(1)}, bf16[128,64]{0,1:T(8,128)(2,1)}, u32[]{:S(2)}) copy-start(bf16[128,64]{0,1:T(8,128)(2,1)} %param.6) | copy-start | bytes 49156
  1.6 1.0 %copy-start = (bf16[128,8,128]{2,1,0:T(8,128)(2,1)S(1)}, bf16[128,8,128]{2,1,0:T(8,128)(2,1)}, u32[]{:S(2)}) copy-start(bf16[128,8,128]{2,1,0:T(8,128)(2,1)} %param.4) | copy-start | bytes 786436

commit v2 on v1

v2 whole, which is shorter than its diff:
```python
import math

import jax
import jax.numpy as jnp
from jax import lax
from jax.experimental import pallas as pl
from jax.experimental.pallas import tpu as pltpu
from jax.sharding import PartitionSpec as P

MESH = pl.DeviceIdType.MESH
NEG = -1e30


def send(s, *jumps):
    return [("send", s, k) for k in jumps]


def swap(first, count):
    return [("swap", first, count)]


def attend(g):
    return [("attend", 4 * g)]


PROGRAM = (
    send(0, 16, 12, 8, 4, 1, 3, 2, 5, 7, 6)
    + send(8, 1, 3, 2) + send(12, 1, 3, 2) + swap(0, 4)
    + send(16, 12, 8, 4, 1, 3, 2, 5, 7, 6)
    + attend(0)
    + swap(4, 4) + attend(1) + swap(8, 8) + attend(2) + attend(3)
    + send(24, 1, 3, 2) + send(28, 1, 3, 2)
    + swap(16, 8) + attend(4) + attend(5)
    + swap(24, 4) + attend(6) + swap(28, 4) + attend(7)
)
SENDS = sum(op[0] == "send" for op in PROGRAM)
SWAPS = sum(op[0] == "swap" for op in PROGRAM)
GROUP = 4


def kernel(
    q_hbm, k_hbm, v_hbm, table_hbm, out_ref,
    q, kv, table, top, acc,
    in_sem, send_sem, recv_sem, swap_send, swap_recv,
):
    h = lax.axis_index("head")
    c = lax.axis_index("ctx")
    core = h % 2
    half = k_hbm.shape[0]
    tokens = k_hbm.shape[1]
    width = 2 * half
    rows = q.shape[0]
    heads = rows // tokens
    stretch = tokens // 2
    factor = width ** (-0.5) * math.log2(math.e)

    own = [
        pltpu.make_async_copy(k_hbm, kv.at[core, 0, pl.ds(0, half)], in_sem.at[0]),
        pltpu.make_async_copy(v_hbm, kv.at[core, 0, pl.ds(half, half)], in_sem.at[1]),
    ]
    later = [
        pltpu.make_async_copy(table_hbm, table, in_sem.at[2]),
        pltpu.make_async_copy(q_hbm, q, in_sem.at[3]),
    ]
    for copy in own + later:
        copy.start()
    jumps = sorted({op[2] for op in PROGRAM if op[0] == "send"}, reverse=True)
    barrier = pltpu.get_barrier_semaphore()
    for k in jumps:
        pl.semaphore_signal(barrier, inc=1, device_id=(h, c ^ k), device_id_type=MESH)
    pl.semaphore_signal(barrier, inc=1, device_id=(h ^ 1, c), device_id_type=MESH)
    for copy in own:
        copy.wait()
    pl.semaphore_wait(barrier, len(jumps) + 1)

    def remote(s, k, i):
        return pltpu.make_async_remote_copy(
            src_ref=kv.at[core, s], dst_ref=kv.at[core, s ^ k],
            send_sem=send_sem.at[i], recv_sem=recv_sem.at[s ^ k],
            device_id=(h, c ^ k), device_id_type=MESH,
        )

    def across(s, n, i, side):
        part = kv.at[side, pl.ds(s, n)]
        return pltpu.make_async_remote_copy(
            src_ref=part, dst_ref=part,
            send_sem=swap_send.at[i], recv_sem=swap_recv.at[i],
            device_id=(h ^ 1, c), device_id_type=MESH,
        )

    def lift(s, i, a):
        return jnp.where(table[i, c ^ s] < table[a, c], jnp.float32(0), jnp.float32(NEG))

    def step(s0):
        slots = range(s0, s0 + GROUP)
        k_t = jnp.concatenate(
            [jnp.concatenate([kv[0, s, :half], kv[1, s, :half]], axis=0) for s in slots], axis=1
        )
        v_t = jnp.concatenate(
            [jnp.concatenate([kv[0, s, half:], kv[1, s, half:]], axis=0) for s in slots], axis=1
        )
        v_t = jnp.concatenate([v_t, jnp.ones((16, v_t.shape[1]), v_t.dtype)], axis=0)
        spans = [slice(a * rows // 2, (a + 1) * rows // 2) for a in range(2)]
        scores = [
            lax.dot_general(
                k_t, q[span, :], (((0,), (1,)), ((), ())), preferred_element_type=jnp.float32
            )
            for span in spans
        ]
        for a, span in enumerate(spans):
            tiles, lifts = [], []
            for n, s in enumerate(slots):
                for i in range(2):
                    at = n * tokens + i * stretch
                    tile = scores[a][at : at + stretch]
                    if s == 0 and i == a:
                        key = lax.broadcasted_iota(jnp.int32, tile.shape, 0)
                        query = lax.broadcasted_iota(jnp.int32, tile.shape, 1) // heads
                        tile = jnp.where(key <= query, tile, NEG)
                        lifts.append(None)
                    else:
                        lifts.append(lift(s, i, a))
                    tiles.append(tile)
            best = None
            for tile, up in zip(tiles, lifts):
                peak = jnp.max(tile.reshape(stretch // 8, 8, rows // 2), axis=0)
                if up is not None:
                    peak = peak + up
                best = peak if best is None else jnp.maximum(best, peak)
            best = jnp.max(best, axis=0, keepdims=True)
            if s0 != 0:
                old = top[0:1, span]
                best = jnp.maximum(old, best)
            weights = [
                jnp.exp2((tile - (best if up is None else best - up)) * factor).astype(kv.dtype)
                for tile, up in zip(tiles, lifts)
            ]
            mixed = jnp.dot(
                v_t, jnp.concatenate(weights, axis=0), preferred_element_type=jnp.float32
            )
            if s0 != 0:
                mixed = acc[:, span] * jnp.exp2((old - best) * factor) + mixed
            acc[:, span] = mixed
            top[0:1, span] = best

    here = {0}

    def arrived(s):
        if s not in here:
            here.add(s)
            remote(s ^ 1, 1, 0).wait_recv()

    sent, swapped, swap_of, pending = [], [], {}, list(later)
    for op in PROGRAM:
        if op[0] == "send":
            arrived(op[1])
            sent.append(remote(op[1], op[2], len(sent)))
            sent[-1].start()
        elif op[0] == "swap":
            for s in range(op[1], op[1] + op[2]):
                arrived(s)
                swap_of[s] = len(swapped)
            swapped.append((op[1], op[2], len(swapped)))
            across(*swapped[-1], core).start()
        else:
            while pending:
                pending.pop().wait()
            i = swap_of[op[1]]
            if i is not None:
                across(*swapped[i], 1 - core).wait_recv()
                for s in swap_of:
                    if swap_of[s] == i:
                        swap_of[s] = None
            step(op[1])

    mix = acc[:width, :] / acc[width : width + 1, :]
    out_ref[...] = mix.T.astype(out_ref.dtype)
    for copy in sent:
        copy.wait_send()
    for part in swapped:
        across(*part, core).wait_send()


def shards(queries, keys, values, stretch_order):
    tokens, heads, width = queries.shape
    rows = tokens * heads
    blocks = lax.axis_size("ctx")
    out = pl.pallas_call(
        kernel,
        out_shape=jax.ShapeDtypeStruct((rows, width), queries.dtype),
        in_specs=[pl.BlockSpec(memory_space=pltpu.HBM)] * 4,
        out_specs=pl.BlockSpec(memory_space=pltpu.VMEM),
        scratch_shapes=[
            pltpu.VMEM((rows, width), queries.dtype),
            pltpu.VMEM((2, blocks, tokens, width), keys.dtype),
            pltpu.SMEM((2, blocks), jnp.int32),
            pltpu.VMEM((8, rows), jnp.float32),
            pltpu.VMEM((width + 16, rows), jnp.float32),
            pltpu.SemaphoreType.DMA((4,)),
            pltpu.SemaphoreType.DMA((SENDS,)),
            pltpu.SemaphoreType.DMA((blocks,)),
            pltpu.SemaphoreType.DMA((SWAPS,)),
            pltpu.SemaphoreType.DMA((SWAPS,)),
        ],
        compiler_params=pltpu.CompilerParams(
            collective_id=0, has_side_effects=True, vmem_limit_bytes=56 * 1024 * 1024
        ),
    )(queries.reshape(rows, width), keys.T, values.T, stretch_order.T)
    return out.reshape(tokens, heads, width)


def solution(mesh):
    in_specs = (P("ctx", "head", None), P("ctx", "head"), P("ctx", "head"), P())
    out_specs = P("ctx", "head", None)
    return jax.shard_map(shards, mesh=mesh, in_specs=in_specs, out_specs=out_specs, check_vma=False)
```

time: 48.4 us -> 37.1 us (0.77)
  the two profiles are of different devices: /device:TPU:66 before, /device:TPU:1 now
where the time goes in v2:
time: 37.1 us; the launch traced here: 36.9 us
  Pallas kernels  35.2 us (95%)
  local copies, waits for them, and re-layouts  1.67 us (5%)
    pallas_call x1, Pallas kernels, shards(): pl.pallas_call(kernel, out_shape=jax.ShapeDtypeStruct((rows, width), quer...  35.2 us
    unnamed x1, local copies, waits for them, and re-layouts  1.67 us

profile of v2, /device:TPU:1, one launch (start us, length us, event | category | flops | bytes accessed | tf_op | source)
XLA Modules:
  0.0 36.9 jit_solution(3913733900881395471)
XLA Ops:
  0.0 35.2 %shard_map.46 = bf16[1024,128]{1,0:T(8,128)(2,1)} custom-call(bf16[1024,128]{1,0:T(8,128)(2,1)} %bitcast.6, bf16[64,128]{1,0:T(8,128)(2,1)} %bitcast.7, bf16[64,128]{1,0:T(8,128)(2,1)} %bitcast.8, s32[2,32]{1,0:T(2,128)} %bitcast.9), custom_call_target="tpu_custom_call" | custom-call | tf_op jit(solution)/shard_map/pallas_call | solution.py:188
  35.2 1.7 %copy.6 = bf16[128,8,128]{2,1,0:T(8,128)(2,1)} copy(bf16[128,8,128]{2,1,0:T(8,128)(2,1)} %bitcast.5) | data formatting | bytes 524288

commit v3 on v2

--- a/solution.py
+++ b/solution.py
@@ -23,13 +23,18 @@
     return [("attend", 4 * g)]
 
 
+FAR = 16
+LATE, EVEN, EARLY = range(3)
 PROGRAM = (
-    send(0, 16, 12, 8, 4, 1, 3, 2, 5, 7, 6)
-    + send(8, 1, 3, 2) + send(12, 1, 3, 2) + swap(0, 4)
+    [("far", LATE), ("near",)]
+    + send(0, 12, 8, 4, 1, 3, 2, 5, 7, 6)
+    + [("far", EVEN)]
+    + send(8, 1, 3, 2) + send(12, 1, 3, 2)
+    + [("far", EARLY)]
     + send(16, 12, 8, 4, 1, 3, 2, 5, 7, 6)
-    + attend(0)
-    + swap(4, 4) + attend(1) + swap(8, 8) + attend(2) + attend(3)
-    + send(24, 1, 3, 2) + send(28, 1, 3, 2)
+    + swap(0, 4) + attend(0) + swap(4, 4) + attend(1)
+    + swap(8, 8) + attend(2)
+    + send(24, 1, 3, 2) + attend(3) + send(28, 1, 3, 2)
     + swap(16, 8) + attend(4) + attend(5)
     + swap(24, 4) + attend(6) + swap(28, 4) + attend(7)
 )
@@ -41,7 +46,7 @@
 def kernel(
     q_hbm, k_hbm, v_hbm, table_hbm, out_ref,
     q, kv, table, top, acc,
-    in_sem, send_sem, recv_sem, swap_send, swap_recv,
+    in_sem, send_sem, recv_sem, swap_send, swap_recv, relay,
 ):
     h = lax.axis_index("head")
     c = lax.axis_index("ctx")
@@ -66,12 +71,34 @@
         copy.start()
     jumps = sorted({op[2] for op in PROGRAM if op[0] == "send"}, reverse=True)
     barrier = pltpu.get_barrier_semaphore()
+
+    def enter(head, ctx):
+        pl.semaphore_signal(barrier, inc=1, device_id=(head, ctx), device_id_type=MESH)
+
+    enter(h - core, c ^ FAR)
     for k in jumps:
-        pl.semaphore_signal(barrier, inc=1, device_id=(h, c ^ k), device_id_type=MESH)
-    pl.semaphore_signal(barrier, inc=1, device_id=(h ^ 1, c), device_id_type=MESH)
+        enter(h - core + 1, c ^ k)
+    enter(h ^ 1, c)
+
+    def entered(counts, n):
+        @pl.when(counts)
+        def _():
+            pl.semaphore_wait(barrier, n + 1)
+            pl.semaphore_signal(relay, inc=1, device_id=(h ^ 1, c), device_id_type=MESH)
+
+        @pl.when(jnp.logical_not(counts))
+        def _():
+            pl.semaphore_wait(relay, 1)
+
     for copy in own:
         copy.wait()
-    pl.semaphore_wait(barrier, len(jumps) + 1)
+    upper_half = c >= FAR
+    first_half = h < 8
+    stands = {
+        LATE: jnp.logical_and(first_half, upper_half),
+        EVEN: jnp.logical_not(first_half),
+        EARLY: jnp.logical_and(first_half, jnp.logical_not(upper_half)),
+    }
 
     def remote(s, k, i):
         return pltpu.make_async_remote_copy(
@@ -152,7 +179,16 @@
 
     sent, swapped, swap_of, pending = [], [], {}, list(later)
     for op in PROGRAM:
-        if op[0] == "send":
+        if op[0] == "near":
+            entered(core == 1, 2 * len(jumps))
+        elif op[0] == "far":
+
+            @pl.when(stands[op[1]])
+            def _():
+                entered(core == 0, 2)
+                remote(0, FAR, SENDS).start()
+
+        elif op[0] == "send":
             arrived(op[1])
             sent.append(remote(op[1], op[2], len(sent)))
             sent[-1].start()
@@ -175,6 +211,7 @@
 
     mix = acc[:width, :] / acc[width : width + 1, :]
     out_ref[...] = mix.T.astype(out_ref.dtype)
+    remote(0, FAR, SENDS).wait_send()
     for copy in sent:
         copy.wait_send()
     for part in swapped:
@@ -185,6 +222,7 @@
     tokens, heads, width = queries.shape
     rows = tokens * heads
     blocks = lax.axis_size("ctx")
+    arrays = (queries.reshape(rows, width), keys.T, values.T, stretch_order.T)
     out = pl.pallas_call(
         kernel,
         out_shape=jax.ShapeDtypeStruct((rows, width), queries.dtype),
@@ -197,15 +235,16 @@
             pltpu.VMEM((8, rows), jnp.float32),
             pltpu.VMEM((width + 16, rows), jnp.float32),
             pltpu.SemaphoreType.DMA((4,)),
-            pltpu.SemaphoreType.DMA((SENDS,)),
+            pltpu.SemaphoreType.DMA((SENDS + 1,)),
             pltpu.SemaphoreType.DMA((blocks,)),
             pltpu.SemaphoreType.DMA((SWAPS,)),
             pltpu.SemaphoreType.DMA((SWAPS,)),
+            pltpu.SemaphoreType.REGULAR,
         ],
         compiler_params=pltpu.CompilerParams(
-            collective_id=0, has_side_effects=True, vmem_limit_bytes=56 * 1024 * 1024
+            collective_id=0, has_side_effects=True, vmem_limit_bytes=48 * 1024 * 1024
         ),
-    )(queries.reshape(rows, width), keys.T, values.T, stretch_order.T)
+    )(*(pltpu.with_memory_space_constraint(x, pltpu.HBM) for x in arrays))
     return out.reshape(tokens, heads, width)
 
 

time: 37.1 us -> 34.2 us (0.922)
  Pallas kernels: 35.2 us -> 33.3 us
  local copies, waits for them, and re-layouts: 1.67 us -> 0.71 us
    pallas_call x1, Pallas kernels: 35.2 us -> 33.3 us  [shards(): pl.pallas_call(kernel, out_shape=jax.ShapeDtypeStruct((rows, width), quer...]
    unnamed x1, local copies, waits for them, and re-layouts: 1.67 us -> 0.71 us
where the time goes in v3:
time: 34.2 us; the launch traced here: 34 us
  Pallas kernels  33.3 us (97%)
  local copies, waits for them, and re-layouts  0.71 us (2%)
    pallas_call x1, Pallas kernels, shards(): pl.pallas_call(kernel, out_shape=jax.ShapeDtypeStruct((rows, width), quer...  33.3 us
    unnamed x1, local copies, waits for them, and re-layouts  0.71 us

profile of v3, /device:TPU:1, one launch (start us, length us, event | category | flops | bytes accessed | tf_op | source)
XLA Modules:
  0.0 34.0 jit_solution(2480187432430650933)
XLA Ops:
  0.0 33.3 %shard_map.46 = bf16[1024,128]{1,0:T(8,128)(2,1)S(1)} custom-call(bf16[1024,128]{1,0:T(8,128)(2,1)} %bitcast.6, bf16[64,128]{1,0:T(8,128)(2,1)} %bitcast.7, bf16[64,128]{1,0:T(8,128)(2,1)} %bitcast.8, s32[2,32]{1,0:T(2,128)} %bitcast.9), custom_call_target="tpu_custom_call" | custom-call | tf_op jit(solution)/shard_map/pallas_call | solution.py:226
  33.3 0.7 %copy.6 = bf16[128,8,128]{2,1,0:T(8,128)(2,1)} copy(bf16[128,8,128]{2,1,0:T(8,128)(2,1)S(1)} %bitcast.5) | data formatting | bytes 524288

commit v4 on v3

--- a/solution.py
+++ b/solution.py
@@ -11,36 +11,24 @@
 NEG = -1e30
 
 
-def send(s, *jumps):
-    return [("send", s, k) for k in jumps]
-
-
-def swap(first, count):
-    return [("swap", first, count)]
-
-
-def attend(g):
-    return [("attend", 4 * g)]
-
-
 FAR = 16
 LATE, EVEN, EARLY = range(3)
 PROGRAM = (
-    [("far", LATE), ("near",)]
-    + send(0, 12, 8, 4, 1, 3, 2, 5, 7, 6)
-    + [("far", EVEN)]
-    + send(8, 1, 3, 2) + send(12, 1, 3, 2)
-    + [("far", EARLY)]
-    + send(16, 12, 8, 4, 1, 3, 2, 5, 7, 6)
-    + swap(0, 4) + attend(0) + swap(4, 4) + attend(1)
-    + swap(8, 8) + attend(2)
-    + send(24, 1, 3, 2) + attend(3) + send(28, 1, 3, 2)
-    + swap(16, 8) + attend(4) + attend(5)
-    + swap(24, 4) + attend(6) + swap(28, 4) + attend(7)
+    ("far", LATE), ("near",), ("send", 0, 12), ("send", 0, 1), ("send", 0, 3), ("send", 0, 8),
+    ("far", EVEN), ("send", 0, 2), ("far", EARLY), ("send", 3, 4), ("send", 8, 2), ("send", 8, 3),
+    ("send", 8, 1), ("swap", 0, 3), ("send", 12, 2), ("send", 12, 1), ("send", 12, 8),
+    ("send", 16, 8), ("send", 16, 4), ("send", 16, 3), ("send", 16, 2), ("send", 1, 4),
+    ("send", 16, 13), ("send", 16, 1), ("send", 12, 3), ("send", 2, 4), ("swap", 3, 1),
+    ("send", 20, 8), ("send", 20, 2), ("send", 20, 3), ("swap", 19, 2), ("send", 19, 12),
+    ("send", 20, 1), ("send", 24, 3), ("send", 24, 2), ("send", 18, 12), ("swap", 11, 5),
+    ("send", 24, 1), ("swap", 16, 3), ("swap", 4, 5), ("swap", 10, 1), ("attend", (1, 3, 0, 2)),
+    ("swap", 9, 1), ("attend", (15, 16, 14, 20)), ("attend", (7, 12, 5, 4)), ("swap", 21, 4),
+    ("attend", (6, 19, 18, 10)), ("swap", 28, 2), ("attend", (13, 9, 11, 8)), ("swap", 25, 3),
+    ("attend", (22, 23, 17, 24)), ("swap", 30, 2), ("attend", (26, 25, 29, 28)),
+    ("attend", (30, 21, 27, 31)),
 )
 SENDS = sum(op[0] == "send" for op in PROGRAM)
 SWAPS = sum(op[0] == "swap" for op in PROGRAM)
-GROUP = 4
 
 
 def kernel(
@@ -118,8 +106,7 @@
     def lift(s, i, a):
         return jnp.where(table[i, c ^ s] < table[a, c], jnp.float32(0), jnp.float32(NEG))
 
-    def step(s0):
-        slots = range(s0, s0 + GROUP)
+    def step(slots, first):
         k_t = jnp.concatenate(
             [jnp.concatenate([kv[0, s, :half], kv[1, s, :half]], axis=0) for s in slots], axis=1
         )
@@ -155,7 +142,7 @@
                     peak = peak + up
                 best = peak if best is None else jnp.maximum(best, peak)
             best = jnp.max(best, axis=0, keepdims=True)
-            if s0 != 0:
+            if not first:
                 old = top[0:1, span]
                 best = jnp.maximum(old, best)
             weights = [
@@ -165,7 +152,7 @@
             mixed = jnp.dot(
                 v_t, jnp.concatenate(weights, axis=0), preferred_element_type=jnp.float32
             )
-            if s0 != 0:
+            if not first:
                 mixed = acc[:, span] * jnp.exp2((old - best) * factor) + mixed
             acc[:, span] = mixed
             top[0:1, span] = best
@@ -178,6 +165,7 @@
             remote(s ^ 1, 1, 0).wait_recv()
 
     sent, swapped, swap_of, pending = [], [], {}, list(later)
+    crossed, attended = set(), ()
     for op in PROGRAM:
         if op[0] == "near":
             entered(core == 1, 2 * len(jumps))
@@ -201,13 +189,12 @@
         else:
             while pending:
                 pending.pop().wait()
-            i = swap_of[op[1]]
-            if i is not None:
-                across(*swapped[i], 1 - core).wait_recv()
-                for s in swap_of:
-                    if swap_of[s] == i:
-                        swap_of[s] = None
-            step(op[1])
+            for s in op[1]:
+                if swap_of[s] not in crossed:
+                    crossed.add(swap_of[s])
+                    across(*swapped[swap_of[s]], 1 - core).wait_recv()
+            step(op[1], not attended)
+            attended += op[1]
 
     mix = acc[:width, :] / acc[width : width + 1, :]
     out_ref[...] = mix.T.astype(out_ref.dtype)

time: 34.2 us -> 29.5 us (0.86)
  the two profiles are of different devices: /device:TPU:1 before, /device:TPU:33 now
where the time goes in v4:
time: 29.5 us; the launch traced here: 29.4 us
  Pallas kernels  28.7 us (97%)
  local copies, waits for them, and re-layouts  0.71 us (2%)
    pallas_call x1, Pallas kernels, shards(): pl.pallas_call(kernel, out_shape=jax.ShapeDtypeStruct((rows, width), quer...  28.7 us
    unnamed x1, local copies, waits for them, and re-layouts  0.71 us

profile of v4, /device:TPU:33, one launch (start us, length us, event | category | flops | bytes accessed | tf_op | source)
XLA Modules:
  0.0 29.4 jit_solution(8139958566956305334)
XLA Ops:
  0.0 28.7 %shard_map.46 = bf16[1024,128]{1,0:T(8,128)(2,1)S(1)} custom-call(bf16[1024,128]{1,0:T(8,128)(2,1)} %bitcast.6, bf16[64,128]{1,0:T(8,128)(2,1)} %bitcast.7, bf16[64,128]{1,0:T(8,128)(2,1)} %bitcast.8, s32[2,32]{1,0:T(2,128)} %bitcast.9), custom_call_target="tpu_custom_call" | custom-call | tf_op jit(solution)/shard_map/pallas_call | solution.py:213
  28.7 0.7 %copy.6 = bf16[128,8,128]{2,1,0:T(8,128)(2,1)} copy(bf16[128,8,128]{2,1,0:T(8,128)(2,1)S(1)} %bitcast.5) | data formatting | bytes 524288

commit v5 on v4

--- a/solution.py
+++ b/solution.py
@@ -11,30 +11,72 @@
 NEG = -1e30
 
 
+LATE, EVEN, EARLY = range(3)
+FACING = (EARLY, EVEN, LATE)
 FAR = 16
-LATE, EVEN, EARLY = range(3)
-PROGRAM = (
-    ("far", LATE), ("near",), ("send", 0, 12), ("send", 0, 1), ("send", 0, 3), ("send", 0, 8),
-    ("far", EVEN), ("send", 0, 2), ("far", EARLY), ("send", 3, 4), ("send", 8, 2), ("send", 8, 3),
-    ("send", 8, 1), ("swap", 0, 3), ("send", 12, 2), ("send", 12, 1), ("send", 12, 8),
-    ("send", 16, 8), ("send", 16, 4), ("send", 16, 3), ("send", 16, 2), ("send", 1, 4),
-    ("send", 16, 13), ("send", 16, 1), ("send", 12, 3), ("send", 2, 4), ("swap", 3, 1),
-    ("send", 20, 8), ("send", 20, 2), ("send", 20, 3), ("swap", 19, 2), ("send", 19, 12),
-    ("send", 20, 1), ("send", 24, 3), ("send", 24, 2), ("send", 18, 12), ("swap", 11, 5),
-    ("send", 24, 1), ("swap", 16, 3), ("swap", 4, 5), ("swap", 10, 1), ("attend", (1, 3, 0, 2)),
-    ("swap", 9, 1), ("attend", (15, 16, 14, 20)), ("attend", (7, 12, 5, 4)), ("swap", 21, 4),
-    ("attend", (6, 19, 18, 10)), ("swap", 28, 2), ("attend", (13, 9, 11, 8)), ("swap", 25, 3),
-    ("attend", (22, 23, 17, 24)), ("swap", 30, 2), ("attend", (26, 25, 29, 28)),
-    ("attend", (30, 21, 27, 31)),
+ATTEND = (
+    (0, 3, 1, 2), (9, 24, 12, 11, 13, 10), (6, 14, 15, 4, 8, 5, 7),
+    (20, 19, 18, 17, 29, 23, 21, 16), (25, 28, 27, 22), (30, 31, 26),
 )
-SENDS = sum(op[0] == "send" for op in PROGRAM)
-SWAPS = sum(op[0] == "swap" for op in PROGRAM)
+ORDERS = (
+    (
+        ("send", 0, 16), ("send", 0, 1), ("send", 0, 8), ("cross", 0, 2), ("send", 0, 2),
+        ("send", 0, 3), ("send", 0, 12), ("cross", 0, 1), ("cross", 8, 2), ("send", 8, 3),
+        ("cross", 12, 3), ("send", 12, 1), ("send", 12, 3), ("send", 8, 2), ("send", 1, 4),
+        ("send", 3, 4), ("send", 16, 8), ("send", 16, 3), ("send", 16, 4), ("send", 8, 1),
+        ("send", 16, 2), ("send", 16, 1), ("send", 16, 13), ("swap", 3, 1), ("send", 16, 12),
+        ("swap", 0, 1), ("send", 7, 1), ("send", 0, 4), ("cross", 13, 3), ("send", 15, 1),
+        ("cross", 20, 3), ("swap", 11, 2), ("swap", 24, 1), ("send", 17, 8), ("swap", 13, 1),
+        ("cross", 24, 3), ("send", 24, 3), ("cross", 20, 1), ("send", 19, 4), ("cross", 19, 12),
+        ("swap", 8, 2), ("send", 20, 1), ("cross", 19, 5), ("attend", 0), ("send", 28, 3),
+        ("cross", 24, 1), ("cross", 24, 2), ("send", 28, 2), ("swap", 4, 4), ("send", 18, 4),
+        ("send", 24, 2), ("swap", 16, 5), ("cross", 18, 12), ("attend", 1), ("swap", 28, 2),
+        ("attend", 2), ("attend", 3), ("attend", 4), ("attend", 5),
+    ),
+    (
+        ("send", 0, 8), ("cross", 0, 2), ("send", 0, 12), ("send", 0, 3), ("send", 0, 7),
+        ("send", 0, 16), ("send", 0, 2), ("send", 0, 1), ("cross", 0, 1), ("send", 8, 2),
+        ("cross", 8, 2), ("cross", 8, 1), ("send", 8, 12), ("send", 12, 3), ("send", 2, 4),
+        ("send", 12, 1), ("send", 12, 2), ("send", 1, 4), ("send", 8, 3), ("send", 16, 4),
+        ("send", 16, 1), ("send", 16, 3), ("send", 16, 8), ("send", 16, 2), ("send", 16, 13),
+        ("swap", 0, 1), ("swap", 3, 6), ("send", 10, 3), ("cross", 20, 2), ("send", 20, 2),
+        ("send", 20, 1), ("swap", 11, 3), ("send", 20, 8), ("send", 24, 3), ("send", 24, 2),
+        ("swap", 24, 1), ("cross", 19, 4), ("cross", 24, 1), ("send", 19, 4), ("cross", 19, 12),
+        ("attend", 0), ("swap", 14, 5), ("cross", 24, 2), ("send", 19, 12), ("cross", 29, 3),
+        ("send", 24, 1), ("send", 29, 3), ("attend", 1), ("swap", 29, 1), ("swap", 19, 3),
+        ("attend", 2), ("swap", 27, 2), ("attend", 3), ("attend", 4), ("attend", 5),
+    ),
+    (
+        ("send", 0, 12), ("send", 0, 8), ("cross", 0, 1), ("send", 0, 3), ("send", 0, 1),
+        ("send", 0, 2), ("send", 0, 16), ("send", 3, 4), ("send", 8, 2), ("send", 8, 1),
+        ("send", 12, 2), ("send", 12, 1), ("send", 8, 12), ("send", 16, 4), ("send", 16, 3),
+        ("swap", 12, 1), ("send", 8, 3), ("send", 16, 8), ("send", 2, 4), ("swap", 2, 2),
+        ("send", 16, 2), ("send", 16, 1), ("send", 16, 13), ("send", 12, 3), ("swap", 0, 1),
+        ("send", 1, 4), ("send", 20, 3), ("send", 20, 2), ("cross", 20, 3), ("cross", 20, 1),
+        ("send", 20, 1), ("send", 19, 12), ("swap", 13, 1), ("cross", 20, 2), ("cross", 24, 1),
+        ("cross", 24, 4), ("swap", 9, 3), ("swap", 24, 1), ("send", 24, 3), ("cross", 24, 3),
+        ("attend", 0), ("swap", 14, 1), ("send", 24, 4), ("swap", 4, 5), ("cross", 18, 12),
+        ("cross", 24, 2), ("swap", 15, 1), ("swap", 18, 3), ("send", 24, 1), ("swap", 16, 2),
+        ("send", 18, 12), ("send", 24, 2), ("attend", 1), ("swap", 29, 1), ("attend", 2),
+        ("swap", 31, 1), ("attend", 3), ("attend", 4), ("attend", 5),
+    ),
+)
+
+
+def jumps(kind, far):
+    found = {op[2] for op in ORDERS[kind] if op[0] in ("send", "cross")}
+    return sorted((k for k in found if (k >= FAR) == far), reverse=True)
+
+
+SENDS = max(sum(op[0] == "send" for op in order) for order in ORDERS)
+CROSSES = max(sum(op[0] == "cross" for op in order) for order in ORDERS)
+SWAPS = max(sum(op[0] == "swap" for op in order) for order in ORDERS)
 
 
 def kernel(
     q_hbm, k_hbm, v_hbm, table_hbm, out_ref,
     q, kv, table, top, acc,
-    in_sem, send_sem, recv_sem, swap_send, swap_recv, relay,
+    in_sem, send_sem, recv_sem, swap_send, swap_recv, cross_send, cross_recv, relay,
 ):
     h = lax.axis_index("head")
     c = lax.axis_index("ctx")
@@ -57,36 +99,44 @@
     ]
     for copy in own + later:
         copy.start()
-    jumps = sorted({op[2] for op in PROGRAM if op[0] == "send"}, reverse=True)
+    upper_half = c >= FAR
+    first_half = h < 8
+    stands = (
+        jnp.logical_and(first_half, upper_half),
+        jnp.logical_not(first_half),
+        jnp.logical_and(first_half, jnp.logical_not(upper_half)),
+    )
+    kinds = range(len(stands))
+
     barrier = pltpu.get_barrier_semaphore()
 
     def enter(head, ctx):
         pl.semaphore_signal(barrier, inc=1, device_id=(head, ctx), device_id_type=MESH)
 
-    enter(h - core, c ^ FAR)
-    for k in jumps:
-        enter(h - core + 1, c ^ k)
     enter(h ^ 1, c)
-
-    def entered(counts, n):
+    for kind in kinds:
+
+        @pl.when(stands[kind])
+        def _(kind=kind):
+            for k in jumps(FACING[kind], True):
+                enter(h - core, c ^ k)
+            for k in jumps(kind, False):
+                enter(h - core + 1, c ^ k)
+
+    for copy in own:
+        copy.wait()
+
+    def entered(kind, far):
+        counts = core == (0 if far else 1)
+
         @pl.when(counts)
         def _():
-            pl.semaphore_wait(barrier, n + 1)
+            pl.semaphore_wait(barrier, 2 * len(jumps(kind, far)) + 1)
             pl.semaphore_signal(relay, inc=1, device_id=(h ^ 1, c), device_id_type=MESH)
 
         @pl.when(jnp.logical_not(counts))
         def _():
             pl.semaphore_wait(relay, 1)
-
-    for copy in own:
-        copy.wait()
-    upper_half = c >= FAR
-    first_half = h < 8
-    stands = {
-        LATE: jnp.logical_and(first_half, upper_half),
-        EVEN: jnp.logical_not(first_half),
-        EARLY: jnp.logical_and(first_half, jnp.logical_not(upper_half)),
-    }
 
     def remote(s, k, i):
         return pltpu.make_async_remote_copy(
@@ -157,52 +207,98 @@
             acc[:, span] = mixed
             top[0:1, span] = best
 
-    here = {0}
-
-    def arrived(s):
-        if s not in here:
-            here.add(s)
+    def over(s, k, i):
+        return pltpu.make_async_remote_copy(
+            src_ref=kv.at[core, s], dst_ref=kv.at[core, s ^ k],
+            send_sem=cross_send.at[i], recv_sem=cross_recv.at[s ^ k],
+            device_id=(h ^ 1, c ^ k), device_id_type=MESH,
+        )
+
+    def came_over(s):
+        part = kv.at[1 - core, s]
+        return pltpu.make_async_remote_copy(
+            src_ref=part, dst_ref=part,
+            send_sem=cross_send.at[0], recv_sem=cross_recv.at[s],
+            device_id=(h ^ 1, c), device_id_type=MESH,
+        )
+
+    here = [{0} for _ in kinds]
+    passed = [[] for _ in kinds]
+    known = [set() for _ in kinds]
+    sent = [[] for _ in kinds]
+    swapped = [[] for _ in kinds]
+    crossed = [set() for _ in kinds]
+
+    def arrived(kind, s):
+        if s not in here[kind]:
+            here[kind].add(s)
             remote(s ^ 1, 1, 0).wait_recv()
 
-    sent, swapped, swap_of, pending = [], [], {}, list(later)
-    crossed, attended = set(), ()
-    for op in PROGRAM:
-        if op[0] == "near":
-            entered(core == 1, 2 * len(jumps))
-        elif op[0] == "far":
-
-            @pl.when(stands[op[1]])
-            def _():
-                entered(core == 0, 2)
-                remote(0, FAR, SENDS).start()
-
-        elif op[0] == "send":
-            arrived(op[1])
-            sent.append(remote(op[1], op[2], len(sent)))
-            sent[-1].start()
-        elif op[0] == "swap":
-            for s in range(op[1], op[1] + op[2]):
-                arrived(s)
-                swap_of[s] = len(swapped)
-            swapped.append((op[1], op[2], len(swapped)))
-            across(*swapped[-1], core).start()
-        else:
-            while pending:
-                pending.pop().wait()
-            for s in op[1]:
-                if swap_of[s] not in crossed:
-                    crossed.add(swap_of[s])
-                    across(*swapped[swap_of[s]], 1 - core).wait_recv()
-            step(op[1], not attended)
-            attended += op[1]
-
-    mix = acc[:width, :] / acc[width : width + 1, :]
-    out_ref[...] = mix.T.astype(out_ref.dtype)
-    remote(0, FAR, SENDS).wait_send()
-    for copy in sent:
-        copy.wait_send()
-    for part in swapped:
-        across(*part, core).wait_send()
+    def meet(kind, far):
+        if far not in known[kind]:
+            known[kind].add(far)
+            entered(kind, far)
+
+    def move(kind, ops):
+        for op in ops:
+            if op[0] == "send":
+                meet(kind, op[2] >= FAR)
+                arrived(kind, op[1])
+                sent[kind].append((op[1], op[2], len(sent[kind])))
+                remote(*sent[kind][-1]).start()
+            elif op[0] == "cross":
+                meet(kind, op[2] >= FAR)
+                arrived(kind, op[1])
+                passed[kind].append((op[1], op[2], len(passed[kind])))
+                over(*passed[kind][-1]).start()
+            elif op[0] == "swap":
+                if not known[kind]:
+                    meet(kind, False)
+                for s in range(op[1], op[1] + op[2]):
+                    arrived(kind, s)
+                swapped[kind].append((op[1], op[2], len(swapped[kind])))
+                across(*swapped[kind][-1], core).start()
+            else:
+                for part in swapped[kind]:
+                    reach = set(range(part[0], part[0] + part[1]))
+                    if part not in crossed[kind] and reach & set(ATTEND[op[1]]):
+                        crossed[kind].add(part)
+                        across(*part, 1 - core).wait_recv()
+                near = {o[1] ^ o[2] for o in ORDERS[kind] if o[0] == "cross" and o[2] < FAR}
+                far = {o[1] ^ o[2] for o in ORDERS[FACING[kind]] if o[0] == "cross" and o[2] >= FAR}
+                for s in ATTEND[op[1]]:
+                    arrived(kind, s)
+                    if s in near | far:
+                        came_over(s).wait_recv()
+
+    starts = [0 for _ in kinds]
+    for i, slots in enumerate(ATTEND):
+        for kind in kinds:
+            end = ORDERS[kind].index(("attend", i)) + 1
+
+            @pl.when(stands[kind])
+            def _(kind=kind, end=end):
+                move(kind, ORDERS[kind][starts[kind] : end])
+
+            starts[kind] = end
+        if i == 0:
+            for copy in later:
+                copy.wait()
+        step(slots, i == 0)
+
+    mix = acc[:width, :] * (1.0 / acc[width : width + 1, :])
+    out_ref[...] = mix.astype(out_ref.dtype).T
+    for kind in kinds:
+
+        @pl.when(stands[kind])
+        def _(kind=kind):
+            move(kind, ORDERS[kind][starts[kind] :])
+            for part in sent[kind]:
+                remote(*part).wait_send()
+            for part in passed[kind]:
+                over(*part).wait_send()
+            for part in swapped[kind]:
+                across(*part, core).wait_send()
 
 
 def shards(queries, keys, values, stretch_order):
@@ -222,10 +318,12 @@
             pltpu.VMEM((8, rows), jnp.float32),
             pltpu.VMEM((width + 16, rows), jnp.float32),
             pltpu.SemaphoreType.DMA((4,)),
-            pltpu.SemaphoreType.DMA((SENDS + 1,)),
+            pltpu.SemaphoreType.DMA((SENDS,)),
             pltpu.SemaphoreType.DMA((blocks,)),
             pltpu.SemaphoreType.DMA((SWAPS,)),
             pltpu.SemaphoreType.DMA((SWAPS,)),
+            pltpu.SemaphoreType.DMA((max(CROSSES, 1),)),
+            pltpu.SemaphoreType.DMA((blocks,)),
             pltpu.SemaphoreType.REGULAR,
         ],
         compiler_params=pltpu.CompilerParams(

time: 29.5 us -> 29.5 us (level)
  the two profiles are of different devices: /device:TPU:33 before, /device:TPU:1 now
where the time goes in v5:
time: 29.5 us; the launch traced here: 29.4 us
  Pallas kernels  28.6 us (97%)
  local copies, waits for them, and re-layouts  0.71 us (2%)
    pallas_call x1, Pallas kernels, shards(): pl.pallas_call(kernel, out_shape=jax.ShapeDtypeStruct((rows, width), quer...  28.6 us
    unnamed x1, local copies, waits for them, and re-layouts  0.71 us

profile of v5, /device:TPU:1, one launch (start us, length us, event | category | flops | bytes accessed | tf_op | source)
XLA Modules:
  0.0 29.4 jit_solution(9104843779236316909)
XLA Ops:
  0.0 28.6 %shard_map.46 = bf16[1024,128]{1,0:T(8,128)(2,1)S(1)} custom-call(bf16[1024,128]{1,0:T(8,128)(2,1)} %bitcast.6, bf16[64,128]{1,0:T(8,128)(2,1)} %bitcast.7, bf16[64,128]{1,0:T(8,128)(2,1)} %bitcast.8, s32[2,32]{1,0:T(2,128)} %bitcast.9), custom_call_target="tpu_custom_call" | custom-call | tf_op jit(solution)/shard_map/pallas_call | solution.py:309
  28.7 0.7 %copy.6 = bf16[128,8,128]{2,1,0:T(8,128)(2,1)} copy(bf16[128,8,128]{2,1,0:T(8,128)(2,1)S(1)} %bitcast.5) | data formatting | bytes 524288

commit v6 on v4

--- a/solution.py
+++ b/solution.py
@@ -24,8 +24,8 @@
     ("send", 24, 1), ("swap", 16, 3), ("swap", 4, 5), ("swap", 10, 1), ("attend", (1, 3, 0, 2)),
     ("swap", 9, 1), ("attend", (15, 16, 14, 20)), ("attend", (7, 12, 5, 4)), ("swap", 21, 4),
     ("attend", (6, 19, 18, 10)), ("swap", 28, 2), ("attend", (13, 9, 11, 8)), ("swap", 25, 3),
-    ("attend", (22, 23, 17, 24)), ("swap", 30, 2), ("attend", (26, 25, 29, 28)),
-    ("attend", (30, 21, 27, 31)),
+    ("attend", (22, 23, 17, 24)), ("swap", 30, 2), ("attend", (26, 25, 29, 28, 21, 27)),
+    ("attend", (30, 31)),
 )
 SENDS = sum(op[0] == "send" for op in PROGRAM)
 SWAPS = sum(op[0] == "swap" for op in PROGRAM)

time: 29.5 us -> 29.5 us (level)
  no operation moved by 1% of the time
where the time goes in v6:
time: 29.5 us; the launch traced here: 29.4 us
  Pallas kernels  28.6 us (97%)
  local copies, waits for them, and re-layouts  0.71 us (2%)
    pallas_call x1, Pallas kernels, shards(): pl.pallas_call(kernel, out_shape=jax.ShapeDtypeStruct((rows, width), quer...  28.6 us
    unnamed x1, local copies, waits for them, and re-layouts  0.71 us

profile of v6, /device:TPU:33, one launch (start us, length us, event | category | flops | bytes accessed | tf_op | source)
XLA Modules:
  0.0 29.4 jit_solution(9736860369313188457)
XLA Ops:
  0.0 28.6 %shard_map.46 = bf16[1024,128]{1,0:T(8,128)(2,1)S(1)} custom-call(bf16[1024,128]{1,0:T(8,128)(2,1)} %bitcast.6, bf16[64,128]{1,0:T(8,128)(2,1)} %bitcast.7, bf16[64,128]{1,0:T(8,128)(2,1)} %bitcast.8, s32[2,32]{1,0:T(2,128)} %bitcast.9), custom_call_target="tpu_custom_call" | custom-call | tf_op jit(solution)/shard_map/pallas_call | solution.py:213
  28.7 0.7 %copy.6 = bf16[128,8,128]{2,1,0:T(8,128)(2,1)} copy(bf16[128,8,128]{2,1,0:T(8,128)(2,1)S(1)} %bitcast.5) | data formatting | bytes 524288
